TPU v7x, 32 devices: a whole 2x2x4 slice. The times are simulated.
32 devices in a mesh: grp: 2 (over core), aux: 4 (over y, x), orb: 4 (over z).
Axes of the slice: x: 2, y: 2, z: 4, core: 2. Of those that a mesh axis runs over, the one named last changes fastest.
Arguments:
- fitted_tensor: bfloat16 [4, 8192, 8192], P('grp', 'aux', 'orb'), may hold values from -0.23925781 to 0.23925781
- block_mask: int32 [2, 64, 64], P('grp'), may hold values 0 or 1
- orbitals: bfloat16 [8192, 256], P('aux'), may hold values from -0.0625 to 0.0625
- nuclear: float32 [8192], replicated, may hold values from 0.5 to 1.5
- centres: float32 [3, 8192], replicated, may hold values from 0 to 8
- mm_positions: float32 [3, 32768], P(None, ('grp', 'aux', 'orb')), may hold values from 0 to 8
- mm_charges: float32 [32768], P(('grp', 'aux', 'orb')), may hold values from -0.12 to 0.12
- neighbours: int32 [32, 2], P(('grp', 'aux', 'orb')), may hold values from 0 to 63, all different within a row
Outputs:
- fock: float32 [8192, 8192], P(('aux', 'orb'))
- mm_potential: float32 [32768], P(('grp', 'aux', 'orb'))
Inputs may be any that keep to these rules, and one draw needn't show every extreme that they name: `neighbours`: each row names 2 different blocks; every block is named by some row.
All inputs are finite; a program needn't handle non-finite values. No bound on the sum of `block_mask` on one device may be relied on, other than what follows from the above.
Results may differ from a plain program's by a relative error of at most 0.01.
Values may be sent and summed in bfloat16 or wider, within the bound.
A program may use at most 128 MiB of HBM per device.

v0:
```python
import jax
import jax.numpy as jnp
from jax import lax
from jax.sharding import PartitionSpec as P

BLK = 128
softening = 1.0


def near_kernel(picker, centre_blocks, charge_blocks, atom_xyz):
    near_xyz = jnp.einsum("kb,cbj->ckj", picker, centre_blocks, precision=lax.Precision.HIGHEST)
    near_xyz = near_xyz.reshape(3, picker.shape[0] * centre_blocks.shape[2])
    near_q = jnp.dot(picker, charge_blocks, precision=lax.Precision.HIGHEST).reshape(-1)
    offsets = near_xyz[:, :, None] - atom_xyz[:, None, :]
    kernel = lax.rsqrt(jnp.sum(offsets * offsets, axis=0) + softening)
    return (kernel, near_q)


def add_diagonal(fock_rows, first_row, field_vec):
    row_count = fock_rows.shape[0]
    values = lax.dynamic_slice_in_dim(field_vec, first_row, row_count, 0)
    row_ids = jnp.arange(row_count, dtype=jnp.int32)[:, None]
    col_ids = jnp.arange(fock_rows.shape[1], dtype=jnp.int32)[None, :]
    on_diagonal = col_ids == first_row + row_ids
    return fock_rows + jnp.where(on_diagonal, values[:, None], jnp.float32(0.0))


def block_picker(first, count, block_total):
    positions = (first + jnp.arange(count, dtype=jnp.int32)) // BLK
    block_ids = jnp.arange(block_total, dtype=jnp.int32)
    return (positions[:, None] == block_ids[None, :]).astype(jnp.float32)


def per_device(
    fitted_tensor, block_mask, orbitals, nuclear, centres, mm_positions, mm_charges, neighbours
):
    row_span = fitted_tensor.shape[1]
    col_span = fitted_tensor.shape[2]
    orb_count = lax.axis_size("orb")
    aux_id = lax.axis_index("aux")
    orb_id = lax.axis_index("orb")
    own_span = row_span // orb_count
    block_total = block_mask.shape[1]
    whole_c = lax.all_gather(orbitals, "aux", axis=0, tiled=True)
    row_start = aux_id * row_span
    col_start = orb_id * col_span
    window_c = lax.dynamic_slice_in_dim(whole_c, col_start, col_span, 0)
    row_pick = block_picker(row_start, row_span, block_total)
    col_pick = block_picker(col_start, col_span, block_total)
    row_bits = jnp.dot(row_pick, block_mask[0].astype(jnp.float32), precision=lax.Precision.HIGHEST)
    mask_wide = jnp.dot(row_bits, col_pick.T, precision=lax.Precision.HIGHEST).astype(jnp.bfloat16)
    masked = fitted_tensor * mask_wide[None]
    x_partial = jnp.einsum("pmn,ni->pmi", masked, window_c, preferred_element_type=jnp.float32)
    x_rows = lax.psum(x_partial, "orb")
    own_rows = lax.dynamic_slice_in_dim(x_rows, orb_id * own_span, own_span, 1)
    x_own = own_rows.astype(jnp.bfloat16)
    own_c = lax.dynamic_slice_in_dim(orbitals, orb_id * own_span, own_span, 0)
    dens_part = 2.0 * jnp.einsum("pmi,mi->p", x_own, own_c, preferred_element_type=jnp.float32)
    densities = lax.psum(dens_part, ("aux", "orb")).astype(jnp.bfloat16)
    coulomb_block = jnp.einsum("pmn,p->mn", masked, densities, preferred_element_type=jnp.float32)
    coulomb = lax.all_to_all(coulomb_block, "orb", split_axis=0, concat_axis=1, tiled=True)
    c_float = whole_c.astype(jnp.float32)
    population = 2.0 * jnp.sum(c_float * c_float, axis=1)
    qm_charge = nuclear - population
    centre_blocks = centres.reshape(3, block_total, BLK)
    charge_blocks = qm_charge.reshape(block_total, BLK)
    picker = (neighbours[0][:, None] == jnp.arange(block_total, dtype=jnp.int32)[None, :]).astype(
        jnp.float32
    )
    kernel, near_q = near_kernel(picker, centre_blocks, charge_blocks, mm_positions)
    mm_potential = jnp.dot(near_q, kernel, precision=lax.Precision.HIGHEST)
    contrib = jnp.dot(kernel, mm_charges, precision=lax.Precision.HIGHEST).reshape(
        picker.shape[0], BLK
    )
    field_part = jnp.dot(picker.T, contrib, precision=lax.Precision.HIGHEST)
    field_sum = lax.psum(field_part, ("grp", "aux", "orb"))
    field_vec = field_sum.reshape(-1)
    own_first = row_start + orb_id * own_span
    exchange_part = jnp.einsum(
        "pmi,pni->mn",
        x_own,
        lax.all_gather(x_own, ("aux", "orb"), axis=1, tiled=True),
        preferred_element_type=jnp.float32,
    )
    fock_part = coulomb - 0.5 * exchange_part
    fock_sum = lax.psum(fock_part, "grp")
    fock = add_diagonal(fock_sum, own_first, field_vec)
    return (fock, mm_potential)


def solution(mesh):
    in_specs = (
        P("grp", "aux", "orb"),
        P("grp", None, None),
        P("aux", None),
        P(),
        P(),
        P(None, ("grp", "aux", "orb")),
        P(("grp", "aux", "orb")),
        P(("grp", "aux", "orb"), None),
    )
    out_specs = (P(("aux", "orb"), None), P(("grp", "aux", "orb")))
    return jax.shard_map(
        per_device, mesh=mesh, in_specs=in_specs, out_specs=out_specs, check_vma=False
    )
```

profile of v0, /device:TPU:0, one launch (start us, length us, event | category | flops | bytes accessed | tf_op | source)
XLA Modules:
  0.0 848.3 jit_solution(9946186388667584154)
XLA Ops:
  7.2 0.0 copy-start
  7.2 0.0 all-gather.3.cloned.1.call-start
  7.2 0.7 all-gather.3.cloned.1.call-update
  8.0 1.0 bitcast_convert_fusion
  9.0 1.7 fusion.6
  10.6 7.5 convolution_convert_fusion
  18.1 14.8 %broadcast_multiply_fusion = bf16[2,2048,2048]{2,1,0:T(8,128)(2,1)} fusion(bf16[2,2048,2048]{2,1,0:T(8,128)(2,1)} %param.8, bf16[2048,2048]{1,0:T(8,128)(2,1)S(1)} %convolution_convert_fusion), kind=kLoop, calls=%fused_computation.7 | loop fusion | flops 8388608 | bytes 41943040 | tf_op jit(solution)/shard_map/mul | solution.py:52
  32.9 32.4 %all-gather.3.cloned.1.call-done = bf16[8192,256]{1,0:T(8,128)(2,1)} async-done(((bf16[2048,256]{1,0:T(8,128)(2,1)}), bf16[8192,256]{1,0:T(8,128)(2,1)}) %all-gather.3.cloned.1.call-update) | async-done | bytes 4194320 | tf_op jit(solution)/shard_map/all_gather | solution.py:44
  65.3 12.5 %fusion.3 = f32[2,2048,256]{2,1,0:T(8,128)} fusion(bf16[2,2048,2048]{2,1,0:T(8,128)(2,1)} %broadcast_multiply_fusion, bf16[8192,256]{1,0:T(8,128)(2,1)} %all-gather.3.cloned.1.call-done, s32[]{:T(128)S(6)} %select_n.32), kind=kOutput, calls=%fused_computation.12 | convolution fusion | flops 4294967296 | bytes 22020100 | tf_op jit(solution)/shard_map/pmn,ni->pmi/dot_general | solution.py:53
  77.8 147.1 %all-reduce.4 = bf16[2,2048,256]{2,1,0:T(8,128)(2,1)S(1)} all-reduce(f32[2,2048,256]{2,1,0:T(8,128)} %fusion.3), channel_id=1, replica_groups=mesh['grp'=2,'aux'=4,'orb'=4] {'orb'}, use_global_device_ids=true, to_apply=%region_0.1 | all-reduce | flops 1048576 | bytes 6291456 | tf_op jit(solution)/shard_map/psum | solution.py:54
  224.9 1.0 multiply_reduce_fusion.2
  225.9 38.2 %psum.29 = bf16[2]{0:T(256)(128)(2,1)S(1)} all-reduce(f32[2]{0:T(128)S(1)} %broadcast_multiply_fusion.1), channel_id=1, replica_groups=mesh['grp'=2,'aux'=4,'orb'=4] {'aux','orb'}, use_global_device_ids=true, to_apply=%region_1.2 | all-reduce | flops 2 | bytes 12 | tf_op jit(solution)/shard_map/psum | solution.py:59
  264.2 28.8 %fusion.1 = f32[1,2048,2048]{2,0,1:T(1,128)S(1)} fusion(bf16[2,2048,2048]{2,1,0:T(8,128)(2,1)} %broadcast_multiply_fusion, bf16[2]{0:T(256)(128)(2,1)S(1)} %psum.29), kind=kOutput, calls=%fused_computation.4 | convolution fusion | flops 16777216 | bytes 33554436 | tf_op jit(solution)/shard_map/pmn,p->mn/dot_general | solution.py:60
  292.9 11.3 %copy.18 = f32[1,2048,2048]{2,1,0:T(8,128)} copy(f32[1,2048,2048]{2,0,1:T(1,128)S(1)} %fusion.1) | data formatting | bytes 33554432 | tf_op jit(solution)/shard_map/pmn,p->mn/dot_general | solution.py:60
  304.2 7.0 all-to-all-start
  311.2 0.0 all-gather.5.cloned.1.call-start
  311.2 0.7 all-gather.5.cloned.1.call-update
  312.0 0.0 all-reduce.3.cloned.1.call-start
  312.0 433.2 %all-to-all-done = f32[4,512,2048]{2,1,0:T(8,128)} async-done(((f32[4,512,2048]{2,1,0:T(8,128)}), f32[4,512,2048]{2,1,0:T(8,128)}, u32[]{:S(2)}, u32[]{:S(2)}) %all-to-all-start) | async-done | bytes 16777248 | tf_op jit(solution)/shard_map/all_to_all | solution.py:61
  745.2 0.0 copy-start.1
  745.2 11.9 %copy.21 = f32[4,64,8,2048]{3,2,0,1:T(8,128)} copy(f32[4,64,8,2048]{3,2,1,0:T(8,128)} %bitcast.23) | data formatting | bytes 33554432 | tf_op jit(solution)/shard_map/all_to_all | solution.py:61
  757.0 0.0 all-gather.5.cloned.1.call-done
  757.0 0.0 copy-done.1
  757.0 14.4 %fusion = f32[512,8192]{1,0:T(8,128)} fusion(f32[512,8192]{1,0:T(8,128)} %bitcast.59, bf16[2,512,256]{2,1,0:T(8,128)(2,1)S(1)} %copy-done.1, bf16[2,8192,256]{2,1,0:T(8,128)(2,1)} %all-gather.5.cloned.1.call-done), kind=kOutput, calls=%fused_computation.1 | convolution fusion | flops 4303355904 | bytes 42467328 | tf_op jit(solution)/shard_map/pmi,pni->mn/dot_general | solution.py:79
  771.4 0.0 copy-start.2
  771.4 0.0 copy-start.5
  771.4 0.0 copy-start.4
  771.4 0.0 copy-start.3
  771.5 0.0 all-reduce.3.cloned.1.call-update
  771.5 0.9 copy-done.2
  772.3 0.0 copy-done.5
  772.3 0.2 convolution_bitcast_fusion.1
  772.5 0.0 copy-done.4
  772.5 0.4 multiply_reduce_fusion.1
  772.9 0.0 copy-done
  772.9 1.0 fusion.8
  773.9 0.3 convolution_bitcast_fusion
  774.2 37.3 %psum.31 = f32[8192]{0:T(1024)S(1)} all-reduce(f32[8192]{0:T(1024)S(1)} %convolution_bitcast_fusion), channel_id=1, replica_groups=mesh['grp'=2,'aux'=4,'orb'=4] {'grp','aux','orb'}, use_global_device_ids=true, to_apply=%region_4.5 | all-reduce | flops 8192 | bytes 65536 | tf_op jit(solution)/shard_map/psum | solution.py:76
  811.5 0.1 dynamic_slice.15
  811.6 3.8 multiply_reduce_fusion
  815.3 0.0 copy-done.3
  815.3 0.2 fusion.15
  815.5 1.3 fusion.7
  816.8 12.9 %all-reduce.3.cloned.1.call-done = f32[512,8192]{1,0:T(8,128)} async-done(((f32[512,8192]{1,0:T(8,128)}), f32[512,8192]{1,0:T(8,128)}) %all-reduce.3.cloned.1.call-update) | async-done | bytes 16777232 | tf_op jit(solution)/shard_map/psum | solution.py:86
  829.7 12.1 %select_add_fusion = f32[512,8192]{1,0:T(8,128)} fusion(f32[512,8192]{1,0:T(8,128)} %all-reduce.3.cloned.1.call-done, f32[512]{0:T(512)S(1)} %dynamic_slice.15, s32[512]{0:T(512)S(1)} %iota_add_fusion.2), kind=kLoop, calls=%fused_computation.2 | loop fusion | flops 12582912 | bytes 33558528 | tf_op jit(solution)/shard_map/add | solution.py:25
  (5 shorter events, 0.0 us)
Async XLA Ops:
  7.2 765.8 %copy-start = (f32[1024]{0:T(1024)S(1)}, f32[1024]{0:T(1024)}, u32[]{:S(2)}) copy-start(f32[1024]{0:T(1024)} %param.14) | copy-start | bytes 12292
  7.2 58.1 %all-gather.3.cloned.1.call-start = ((), (), s32[]{:S(2)}) async-start(), calls=%async_computation.1 | async-start | bytes 5242880 | tf_op jit(solution)/shard_map/all_gather | solution.py:44
  304.2 440.9 %all-to-all-start = ((f32[4,512,2048]{2,1,0:T(8,128)}), f32[4,512,2048]{2,1,0:T(8,128)}, u32[]{:S(2)}, u32[]{:S(2)}) async-start(f32[4,512,2048]{2,1,0:T(8,128)} %bitcast.58), calls=%async_computation | async-start | bytes 33554432 | tf_op jit(solution)/shard_map/all_to_all | solution.py:61
  311.2 445.8 %all-gather.5.cloned.1.call-start = ((), (), s32[]{:S(2)}) async-start(), calls=%async_computation.2 | async-start | bytes 8912896 | tf_op jit(solution)/shard_map/all_gather | solution.py:82
  312.0 517.8 %all-reduce.3.cloned.1.call-start = ((), (), s32[]{:S(2)}) async-start(), calls=%async_computation.3 | async-start | bytes 33554432 | tf_op jit(solution)/shard_map/psum | solution.py:86
  745.2 11.9 %copy-start.1 = (bf16[2,512,256]{2,1,0:T(8,128)(2,1)S(1)}, bf16[2,512,256]{2,1,0:T(8,128)(2,1)}, u32[]{:S(2)}) copy-start(bf16[2,512,256]{2,1,0:T(8,128)(2,1)} %get-tuple-element.3) | copy-start | bytes 1572868
  771.4 0.9 copy-start.2
  771.4 0.9 copy-start.5
  771.4 1.1 copy-start.4
  771.4 43.9 %copy-start.3 = (f32[8192]{0:T(1024)S(1)}, f32[8192]{0:T(1024)}, u32[]{:S(2)}) copy-start(f32[8192]{0:T(1024)} %param.11) | copy-start | bytes 98308
Sparse Core Ops, SparseCore 0:
  9.9 55.3 all-gather.2
  314.8 381.6 all-gather.4
  771.6 58.0 all-reduce.2
where the time goes:
time: 849 us; the launch traced here: 848 us
  waiting for transfers between devices  480 us (57%)
  blocking collectives  223 us (26%)
  matrix products  67.7 us (8%)
  other arithmetic  33.1 us (4%)
  local copies, waits for them, and re-layouts  24.2 us (3%)
  between operations  13.9 us (2%)
    all_to_all x1, waiting for transfers between devices, per_device(): lax.all_to_all(coulomb_block, 'orb', split_axis=0, concat_axis=1, tiled=T...  433 us
    psum x1, blocking collectives, per_device(): x_rows = lax.psum(x_partial, 'orb')  147 us
    psum x1, blocking collectives, per_device(): densities = lax.psum(dens_part, ('aux', 'orb')).astype(jnp.bfloat16)  38.2 us
    psum x1, blocking collectives, per_device(): field_sum = lax.psum(field_part, ('grp', 'aux', 'orb'))  37.3 us
    all_gather x1, waiting for transfers between devices, per_device(): whole_c = lax.all_gather(orbitals, 'aux', axis=0, tiled=True)  32.4 us
    dot_general x1, matrix products, per_device(): jnp.einsum('pmn,p->mn', masked, densities, preferred_element_type=jnp.flo...  28.8 us
  transfers between devices with their start and end apart: 4, of which 3 were waited for; matrix products, arithmetic and copies ran while one was open for 5% of the time, Pallas kernels for 0%

commit v1 on v0

--- a/solution.py
+++ b/solution.py
@@ -58,7 +58,12 @@
     dens_part = 2.0 * jnp.einsum("pmi,mi->p", x_own, own_c, preferred_element_type=jnp.float32)
     densities = lax.psum(dens_part, ("aux", "orb")).astype(jnp.bfloat16)
     coulomb_block = jnp.einsum("pmn,p->mn", masked, densities, preferred_element_type=jnp.float32)
-    coulomb = lax.all_to_all(coulomb_block, "orb", split_axis=0, concat_axis=1, tiled=True)
+    coulomb = jnp.concatenate(
+        lax.all_to_all(
+            jnp.stack(jnp.split(coulomb_block, lax.axis_size("orb"), axis=0)), "orb", 0, 0
+        ),
+        axis=1,
+    )
     c_float = whole_c.astype(jnp.float32)
     population = 2.0 * jnp.sum(c_float * c_float, axis=1)
     qm_charge = nuclear - population

time: 849 us -> 917 us (1.080)
  matrix products: 67.7 us -> 121 us
  other arithmetic: 33.1 us -> 43.9 us
    dot_general x1, matrix products: 28.8 us -> 81.8 us  [per_device(): jnp.einsum('pmn,p->mn', masked, densities, preferred_element_type=jnp.flo...]
    all_to_all x1 -> x0, local copies, waits for them, and re-layouts: 11.9 us -> none  [per_device(): lax.all_to_all(coulomb_block, 'orb', split_axis=0, concat_axis=1, tiled=T...]
    reshape x0 -> x1, local copies, waits for them, and re-layouts: none -> 11.9 us  [per_device(): jnp.concatenate(lax.all_to_all(jnp.stack(jnp.split(coulomb_block, lax.axi...]
    another operation x0 -> x1, other arithmetic: none -> 10.9 us  [per_device(): jnp.stack(jnp.split(coulomb_block, lax.axis_size('orb'), axis=0))]
where the time goes in v1:
time: 917 us
  waiting for transfers between devices  480 us (52%)
  blocking collectives  222 us (24%)
  matrix products  121 us (13%)
  other arithmetic  43.9 us (5%)
  local copies, waits for them, and re-layouts  28.5 us (3%)
  between operations  13.9 us (2%)
    all_to_all x1, waiting for transfers between devices, per_device(): lax.all_to_all(jnp.stack(jnp.split(coulomb_block, lax.axis_size('orb'), a...  433 us
    psum x1, blocking collectives, per_device(): x_rows = lax.psum(x_partial, 'orb')  147 us
    dot_general x1, matrix products, per_device(): jnp.einsum('pmn,p->mn', masked, densities, preferred_element_type=jnp.flo...  81.8 us
    psum x1, blocking collectives, per_device(): densities = lax.psum(dens_part, ('aux', 'orb')).astype(jnp.bfloat16)  38.2 us
    psum x1, blocking collectives, per_device(): field_sum = lax.psum(field_part, ('grp', 'aux', 'orb'))  37.1 us
    all_gather x1, waiting for transfers between devices, per_device(): whole_c = lax.all_gather(orbitals, 'aux', axis=0, tiled=True)  32.4 us
  transfers between devices with their start and end apart: 4, of which 3 were waited for; matrix products, arithmetic and copies ran while one was open for 5% of the time, Pallas kernels for 0%

profile of v1, /device:TPU:0, one launch (start us, length us, event | category | flops | bytes accessed | tf_op | source)
XLA Modules:
  0.0 916.6 jit_solution(322418526010316319)
XLA Ops:
  7.2 0.0 copy-start
  7.2 0.0 all-gather.3.cloned.1.call-start
  7.2 0.7 all-gather.3.cloned.1.call-update
  8.0 1.0 bitcast_convert_fusion
  9.0 1.7 fusion.6
  10.6 7.5 convolution_convert_fusion
  18.1 14.8 %broadcast_multiply_fusion = bf16[2,2048,2048]{2,1,0:T(8,128)(2,1)} fusion(bf16[2,2048,2048]{2,1,0:T(8,128)(2,1)} %param.8, bf16[2048,2048]{1,0:T(8,128)(2,1)S(1)} %convolution_convert_fusion), kind=kLoop, calls=%fused_computation.9 | loop fusion | flops 8388608 | bytes 41943040 | tf_op jit(solution)/shard_map/mul | solution.py:52
  32.9 32.4 %all-gather.3.cloned.1.call-done = bf16[8192,256]{1,0:T(8,128)(2,1)} async-done(((bf16[2048,256]{1,0:T(8,128)(2,1)}), bf16[8192,256]{1,0:T(8,128)(2,1)}) %all-gather.3.cloned.1.call-update) | async-done | bytes 4194320 | tf_op jit(solution)/shard_map/all_gather | solution.py:44
  65.3 12.5 %fusion.3 = f32[2,2048,256]{2,1,0:T(8,128)} fusion(bf16[2,2048,2048]{2,1,0:T(8,128)(2,1)} %broadcast_multiply_fusion, bf16[8192,256]{1,0:T(8,128)(2,1)} %all-gather.3.cloned.1.call-done, s32[]{:T(128)S(6)} %select_n.32), kind=kOutput, calls=%fused_computation.18 | convolution fusion | flops 4294967296 | bytes 22020100 | tf_op jit(solution)/shard_map/pmn,ni->pmi/dot_general | solution.py:53
  77.8 147.1 %all-reduce.4 = bf16[2,2048,256]{2,1,0:T(8,128)(2,1)S(1)} all-reduce(f32[2,2048,256]{2,1,0:T(8,128)} %fusion.3), channel_id=1, replica_groups=mesh['grp'=2,'aux'=4,'orb'=4] {'orb'}, use_global_device_ids=true, to_apply=%region_0.1 | all-reduce | flops 1048576 | bytes 6291456 | tf_op jit(solution)/shard_map/psum | solution.py:54
  224.9 1.0 multiply_reduce_fusion.2
  225.9 38.2 %psum.29 = bf16[2]{0:T(256)(128)(2,1)S(1)} all-reduce(f32[2]{0:T(128)S(1)} %broadcast_multiply_fusion.1), channel_id=1, replica_groups=mesh['grp'=2,'aux'=4,'orb'=4] {'aux','orb'}, use_global_device_ids=true, to_apply=%region_1.2 | all-reduce | flops 2 | bytes 12 | tf_op jit(solution)/shard_map/psum | solution.py:59
  264.2 81.8 %fusion.1 = f32[1,2048,2048]{2,0,1:T(1,128)} fusion(bf16[2,2048,2048]{2,1,0:T(8,128)(2,1)} %broadcast_multiply_fusion, bf16[2]{0:T(256)(128)(2,1)S(1)} %psum.29), kind=kOutput, calls=%fused_computation.6 | convolution fusion | flops 16777216 | bytes 33554436 | tf_op jit(solution)/shard_map/pmn,p->mn/dot_general | solution.py:60
  346.0 11.0 %copy.35 = f32[1,2048,2048]{2,1,0:T(8,128)S(1)} copy(f32[1,2048,2048]{2,0,1:T(1,128)} %fusion.1) | data formatting | bytes 33554432 | tf_op jit(solution)/shard_map/pmn,p->mn/dot_general | solution.py:60
  357.0 4.6 slice_bitcast_fusion.3
  361.6 10.9 %pad_maximum_fusion = f32[4,512,2048]{2,1,0:T(8,128)} fusion(f32[1,512,2048]{2,1,0:T(8,128)} %get-tuple-element.5, f32[1,512,2048]{2,1,0:T(8,128)} %get-tuple-element.6, f32[1,512,2048]{2,1,0:T(8,128)} %get-tuple-element.7, f32[1,512,2048]{2,1,0:T(8,128)S(1)} %get-tuple-element.4), kind=kLoop, calls=%fused_computation | loop fusion | flops 12582912 | bytes 33554432 | tf_op jit(solution)/shard_map/stack | solution.py:63
  372.4 7.0 all-to-all-start
  379.4 0.0 all-gather.5.cloned.1.call-start
  379.5 0.7 all-gather.5.cloned.1.call-update
  380.2 0.3 all-reduce.3.cloned.1.call-start
  380.4 432.9 %all-to-all-done = f32[4,512,2048]{2,1,0:T(8,128)} async-done(((f32[4,512,2048]{2,1,0:T(8,128)}), f32[4,512,2048]{2,1,0:T(8,128)}, u32[]{:S(2)}, u32[]{:S(2)}) %all-to-all-start) | async-done | bytes 16777248 | tf_op jit(solution)/shard_map/all_to_all | solution.py:62
  813.4 0.0 copy-start.1
  813.4 11.9 %copy.24 = f32[4,64,8,2048]{3,2,0,1:T(8,128)} copy(f32[4,64,8,2048]{3,2,1,0:T(8,128)} %bitcast.25) | data formatting | bytes 33554432 | tf_op jit(solution)/shard_map/reshape | solution.py:61
  825.2 0.0 all-gather.5.cloned.1.call-done
  825.3 0.0 copy-done.1
  825.3 14.4 %fusion = f32[512,8192]{1,0:T(8,128)} fusion(f32[512,8192]{1,0:T(8,128)} %bitcast.67, bf16[2,512,256]{2,1,0:T(8,128)(2,1)S(1)} %copy-done.1, bf16[2,8192,256]{2,1,0:T(8,128)(2,1)} %all-gather.5.cloned.1.call-done), kind=kOutput, calls=%fused_computation.2 | convolution fusion | flops 4303355904 | bytes 42467328 | tf_op jit(solution)/shard_map/pmi,pni->mn/dot_general | solution.py:84
  839.6 0.0 copy-start.2
  839.6 0.0 copy-start.5
  839.6 0.0 copy-start.4
  839.6 0.0 copy-start.3
  839.7 0.0 all-reduce.3.cloned.1.call-update
  839.7 0.9 copy-done.2
  840.5 0.0 copy-done.5
  840.5 0.2 convolution_bitcast_fusion.1
  840.7 0.0 copy-done.4
  840.8 0.4 multiply_reduce_fusion.1
  841.1 0.0 copy-done
  841.1 1.0 fusion.8
  842.1 0.3 convolution_bitcast_fusion
  842.4 37.1 %psum.31 = f32[8192]{0:T(1024)S(1)} all-reduce(f32[8192]{0:T(1024)S(1)} %convolution_bitcast_fusion), channel_id=1, replica_groups=mesh['grp'=2,'aux'=4,'orb'=4] {'grp','aux','orb'}, use_global_device_ids=true, to_apply=%region_4.5 | all-reduce | flops 8192 | bytes 65536 | tf_op jit(solution)/shard_map/psum | solution.py:81
  879.5 0.1 dynamic_slice.15
  879.6 3.7 multiply_reduce_fusion
  883.3 0.0 copy-done.3
  883.3 0.2 fusion.15
  883.5 1.3 fusion.7
  884.7 13.2 %all-reduce.3.cloned.1.call-done = f32[512,8192]{1,0:T(8,128)} async-done(((f32[512,8192]{1,0:T(8,128)}), f32[512,8192]{1,0:T(8,128)}) %all-reduce.3.cloned.1.call-update) | async-done | bytes 16777232 | tf_op jit(solution)/shard_map/psum | solution.py:91
  898.0 12.1 %select_add_fusion = f32[512,8192]{1,0:T(8,128)} fusion(f32[512,8192]{1,0:T(8,128)} %all-reduce.3.cloned.1.call-done, f32[512]{0:T(512)S(1)} %dynamic_slice.15, s32[512]{0:T(512)S(1)} %iota_add_fusion.2), kind=kLoop, calls=%fused_computation.4 | loop fusion | flops 12582912 | bytes 33558528 | tf_op jit(solution)/shard_map/add | solution.py:25
  (5 shorter events, 0.0 us)
Async XLA Ops:
  7.2 834.0 %copy-start = (f32[1024]{0:T(1024)S(1)}, f32[1024]{0:T(1024)}, u32[]{:S(2)}) copy-start(f32[1024]{0:T(1024)} %param.14) | copy-start | bytes 12292
  7.2 58.1 %all-gather.3.cloned.1.call-start = ((), (), s32[]{:S(2)}) async-start(), calls=%async_computation.1 | async-start | bytes 5242880 | tf_op jit(solution)/shard_map/all_gather | solution.py:44
  372.4 440.9 %all-to-all-start = ((f32[4,512,2048]{2,1,0:T(8,128)}), f32[4,512,2048]{2,1,0:T(8,128)}, u32[]{:S(2)}, u32[]{:S(2)}) async-start(f32[4,512,2048]{2,1,0:T(8,128)} %pad_maximum_fusion), calls=%async_computation | async-start | bytes 33554432 | tf_op jit(solution)/shard_map/all_to_all | solution.py:62
  379.4 445.8 %all-gather.5.cloned.1.call-start = ((), (), s32[]{:S(2)}) async-start(), calls=%async_computation.2 | async-start | bytes 8912896 | tf_op jit(solution)/shard_map/all_gather | solution.py:87
  380.2 517.8 %all-reduce.3.cloned.1.call-start = ((), (), s32[]{:S(2)}) async-start(), calls=%async_computation.3 | async-start | bytes 33554432 | tf_op jit(solution)/shard_map/psum | solution.py:91
  813.4 11.9 %copy-start.1 = (bf16[2,512,256]{2,1,0:T(8,128)(2,1)S(1)}, bf16[2,512,256]{2,1,0:T(8,128)(2,1)}, u32[]{:S(2)}) copy-start(bf16[2,512,256]{2,1,0:T(8,128)(2,1)} %get-tuple-element.3) | copy-start | bytes 1572868
  839.6 0.9 copy-start.2
  839.6 0.9 copy-start.5
  839.6 1.1 copy-start.4
  839.6 43.6 %copy-start.3 = (f32[8192]{0:T(1024)S(1)}, f32[8192]{0:T(1024)}, u32[]{:S(2)}) copy-start(f32[8192]{0:T(1024)} %param.11) | copy-start | bytes 98308
Sparse Core Ops, SparseCore 0:
  9.9 55.3 all-gather.2
  383.0 381.6 all-gather.4
  839.8 58.1 all-reduce.2
